TPU v7x, 256 devices: a whole 4x4x8 slice. The times are simulated.
256 devices in a mesh: dom: 64 (over y, z, core), rep: 4 (over x).
Axes of the slice: x: 4, y: 4, z: 8, core: 2. Of those that a mesh axis runs over, the one named last changes fastest.
Arguments:
- features: bfloat16 [131072, 256], P('dom', 'rep'), may hold values from -6 to 6
- order: int32 [64, 2048], P('dom'), may hold values from 0 to 2047, each once within a row
- weight: bfloat16 [256, 256], P('rep'), may hold values from -0.375 to 0.375
- bias: float32 [256], P('rep'), may hold values from -3 to 3
- tiles: bfloat16 [1024, 8, 128, 128], P('dom'), may hold values from -0.375 to 0.375
- col_ids: int32 [1024, 8], P('dom'), may hold values from 0 to 1023, as said below
- counts: int32 [1024], P('dom'), may hold values from 1 to 8, as said below
Outputs:
- activated: bfloat16 [131072, 256], P('dom', 'rep')
Inputs may be any that keep to these rules, and one draw needn't show every extreme that they name: `col_ids`: block i belongs to index i // 16 of dom. Among the 128 slots of one index of dom, at most 2 name blocks of any one index, and some reach 2. `counts`: slots at or beyond the count are ignored. Every index of dom has a block row with 8.
All inputs are finite; a program needn't handle non-finite values.
Results may differ from a plain program's by a relative error of at most 0.0047.
Values may be sent and summed in bfloat16 or wider, within the bound.
No kernel may reach another device: no remote copies, remote signals or barrier semaphores. Data moves between devices by JAX's collectives and lax.ppermute only.
A program may use at most 128 MiB of HBM per device.

v0:
```python
import functools

import jax
import jax.numpy as jnp
from jax import lax
from jax.experimental import pallas as pl
from jax.experimental.pallas import tpu as pltpu
from jax.sharding import PartitionSpec as P

VMEM_LIMIT = 24 * 1024 * 1024
VMEM = pl.BlockSpec(memory_space=pltpu.VMEM)
SMEM = pl.BlockSpec(memory_space=pltpu.SMEM)
Y, Z, CORES = 4, 8, 2
CHUNKS = ((0, -1), (1, -2, 2), (-3, 3), (4,))


def hidden_kernel(rep_ref, order_ref, x0_ref, x1_ref, x2_ref, x3_ref, blocks_ref):
    width = x0_ref.shape[0]
    count, _, size = blocks_ref.shape
    nodes = count * size
    rep = rep_ref[0]
    weights = []
    features = []
    for part in (x0_ref, x1_ref, x2_ref, x3_ref):
        columns = part[:, nodes : nodes + width]
        for index in range(1, (part.shape[1] - nodes) // width):
            other = part[:, nodes + index * width : nodes + (index + 1) * width]
            columns = jnp.where(rep == index, other, columns)
        weights.append(columns)
        features.append(part[:, :nodes])
    total = lax.dot_general(
        jnp.concatenate(weights, axis=0),
        jnp.concatenate(features, axis=0),
        (((0,), (0,)), ((), ())),
        preferred_element_type=jnp.float32,
    )
    hidden = total.astype(jnp.bfloat16).astype(jnp.float32)
    for block in range(count):
        order = order_ref[:, block * size : (block + 1) * size]
        order = jnp.broadcast_to(order, (width, size))
        lane = jnp.bitwise_and(order, size - 1)
        chunk = lax.shift_right_logical(order, size.bit_length() - 1)
        value = jnp.zeros((width, size), jnp.float32)
        for source in range(count):
            piece = hidden[:, source * size : (source + 1) * size]
            picked = jnp.take_along_axis(piece, lane, axis=1)
            value = jnp.where(chunk == source, picked, value)
        blocks_ref[block] = value.astype(jnp.bfloat16)


def make_hidden(rep, order, parts, width, nodes, size):
    return pl.pallas_call(
        hidden_kernel,
        out_shape=jax.ShapeDtypeStruct((nodes // size, width, size), jnp.bfloat16),
        in_specs=[SMEM] + [VMEM] * (1 + len(parts)),
        out_specs=VMEM,
        compiler_params=pltpu.CompilerParams(vmem_limit_bytes=VMEM_LIMIT),
        cost_estimate=pl.CostEstimate(flops=400_000_000, bytes_accessed=8_000_000, transcendentals=0),
        name="hidden_blocks",
    )(rep, order, *parts)


def pick_kernel(near, count, request_ref, place_ref, *refs):
    own_ref, core_ref, *send_refs = refs[-(1 + Y) :]
    sources = refs[: -(1 + Y)]
    y, z, core = place_ref[0], place_ref[1], place_ref[2]
    half = count // 2

    def block(index, wanted):
        if index < len(near) - 1 or near[index] != Z // 2:
            return sources[index][wanted]
        low = sources[index][jnp.minimum(wanted, half - 1)]
        high = sources[index + 1][jnp.maximum(wanted - half, 0)]
        return jnp.where(wanted < half, low, high)

    for shift in range(Y):
        for other in range(CORES):
            row = lax.rem(y + shift, Y) * CORES + jnp.bitwise_xor(core, other)
            for index, offset in enumerate(near):
                owner = lax.rem(z + offset * (1 - jnp.bitwise_and(z, 1) * 2) + Z, Z)
                for slot in range(2):
                    wanted = jnp.bitwise_and(request_ref[row, owner * 2 + slot], count - 1)
                    value = block(index, wanted)
                    if shift:
                        send_refs[shift - 1][other, index, slot] = value
                    elif other:
                        core_ref[index, slot] = value
                    else:
                        own_ref[index, slot] = value


def make_pick(near, count, request, place, sources):
    piece = sources[0].shape[1:]
    one = jax.ShapeDtypeStruct((len(near), 2) + piece, jnp.bfloat16)
    both = jax.ShapeDtypeStruct((CORES, len(near), 2) + piece, jnp.bfloat16)
    return pl.pallas_call(
        functools.partial(pick_kernel, near, count),
        out_shape=(one, one) + (both,) * (Y - 1),
        in_specs=[SMEM, SMEM] + [VMEM] * len(sources),
        out_specs=(VMEM,) * (1 + Y),
        compiler_params=pltpu.CompilerParams(vmem_limit_bytes=VMEM_LIMIT),
        name="pick_blocks",
    )(request, place, *sources)


def sum_kernel(where_ref, tiles_ref, bias_ref, *refs):
    *parts, out_ref, got_ref = refs
    start = 0
    for chunk in range(0, len(parts), Y + 1):
        own_ref, *arrived, swapped_ref = parts[chunk : chunk + Y + 1]
        pairs = own_ref.shape[0]
        for shift in range(Y):
            for other in range(CORES):
                base = (shift * CORES + other) * Z * 2 + start
                for pair in range(pairs):
                    for slot in range(2):
                        if other:
                            value = swapped_ref[shift, pair, slot]
                        elif shift:
                            value = arrived[shift - 1][0, pair, slot]
                        else:
                            value = own_ref[pair, slot]
                        got_ref[base + pair * 2 + slot] = value
        start += pairs * 2
    rows, slots, size, _ = tiles_ref.shape
    for row in range(rows):
        pieces = [got_ref[where_ref[row * slots + slot]] for slot in range(slots)]
        gathered = jnp.concatenate(pieces, axis=1)
        tiles = jnp.concatenate([tiles_ref[row, slot] for slot in range(slots)], axis=1)
        summed = lax.dot_general(
            gathered, tiles, (((1,), (1,)), ((), ())), preferred_element_type=jnp.float32
        )
        out_ref[:, row * size : (row + 1) * size] = jnp.maximum(
            summed + bias_ref[...], 0.0
        ).astype(out_ref.dtype)


def make_sum(where, tiles, bias, parts):
    rows, slots, size, _ = tiles.shape
    width = bias.shape[0]
    return pl.pallas_call(
        sum_kernel,
        out_shape=jax.ShapeDtypeStruct((width, rows * size), jnp.bfloat16),
        in_specs=[SMEM, VMEM, VMEM] + [VMEM] * len(parts),
        out_specs=VMEM,
        scratch_shapes=[pltpu.VMEM((rows * slots, width, size), jnp.bfloat16)],
        compiler_params=pltpu.CompilerParams(vmem_limit_bytes=VMEM_LIMIT),
        name="sum_tiles",
    )(where, tiles, bias, *parts)


def load_kernel(counts_ref, tiles_ref, used_ref):
    rows, slots = tiles_ref.shape[:2]

    def load(row, carry):
        for slot in range(slots):
            tile = tiles_ref[row, slot]
            used_ref[row, slot] = jnp.where(slot < counts_ref[row], tile, jnp.zeros_like(tile))
        return carry

    lax.fori_loop(0, rows, load, 0, unroll=2)


def make_load(counts, tiles):
    return pl.pallas_call(
        load_kernel,
        out_shape=jax.ShapeDtypeStruct(tiles.shape, tiles.dtype),
        in_specs=[SMEM, VMEM],
        out_specs=VMEM,
        compiler_params=pltpu.CompilerParams(vmem_limit_bytes=VMEM_LIMIT),
        cost_estimate=pl.CostEstimate(flops=0, bytes_accessed=8_000_000, transcendentals=0),
        name="load_tiles",
    )(counts, tiles)


def dom_index(y, z, core):
    return (y * Z + z) * CORES + core


def move(array, shift_y, side, other):
    pairs = [
        (
            dom_index(y, z, core),
            dom_index((y + shift_y) % Y, (z + side * (1 - z % 2 * 2)) % Z, core ^ other),
        )
        for y in range(Y)
        for z in range(Z)
        for core in range(CORES)
    ]
    return lax.ppermute(array, "dom", pairs)


def body(features, order, weight, bias, tiles, col_ids, counts):
    nodes, width = features.shape
    rows, slots, size, _ = tiles.shape
    reps = lax.axis_size("rep")
    rep = lax.axis_index("rep").astype(jnp.int32)
    dom = lax.axis_index("dom").astype(jnp.int32)
    y, z, core = dom // (Z * CORES), (dom // CORES) % Z, dom % CORES
    mine = jnp.concatenate([features.T, weight], axis=1)
    parts = [mine] + [
        lax.ppermute(mine, "rep", [(i, (i + shift) % reps) for i in range(reps)])
        for shift in range(1, reps)
    ]

    ids = col_ids.reshape(-1)
    total = ids.shape[0]
    owner = ids // rows
    slot = jnp.arange(total, dtype=jnp.int32)
    code = slot * rows + ids % rows
    row = lax.broadcasted_iota(jnp.int32, (Y * CORES, 128), 0)
    lane = lax.broadcasted_iota(jnp.int32, (Y * CORES, 128), 1)
    asked = dom_index(row // CORES, (lane // 2) % Z, row % CORES)
    match = owner[None, None, :] == asked[:, :, None]
    first = jnp.min(jnp.where(match, code[None, None, :], total * rows), axis=2)
    last = jnp.max(jnp.where(match, code[None, None, :], -1), axis=2)
    request = jnp.where(lane % 2 == 0, first, last) % rows
    groups = [
        [dom_index(group_y, group_z, group_core) for group_y in range(Y) for group_core in range(CORES)]
        for group_z in range(Z)
    ]
    request = lax.all_to_all(request, "dom", 0, 0, axis_index_groups=groups, tiled=True)

    earlier = (owner[None, :] == owner[:, None]) & (slot[None, :] < slot[:, None])
    rank = jnp.any(earlier, axis=1).astype(jnp.int32)
    away = ((owner // CORES) % Z - z) * (1 - z % 2 * 2) % Z
    found = jnp.zeros_like(away)
    for index, offset in enumerate(sum(CHUNKS, ())):
        found = jnp.where(away == offset % Z, index, found)
    shift = (y - owner // (Z * CORES)) % Y
    other = jnp.bitwise_xor(owner % CORES, core)
    where = ((shift * CORES + other) * Z + found) * 2 + rank

    order = jnp.bitwise_and(order, nodes - 1)
    request, order, *parts = lax.optimization_barrier((request, order, *parts))
    blocks = make_hidden(rep[None], order, parts, width, nodes, size)
    ups, downs = [blocks, move(blocks, 0, 1, 0)], [blocks, move(blocks, 0, -1, 0)]
    used = make_load(counts, tiles)
    ups[1], downs[1], used = lax.optimization_barrier((ups[1], downs[1], used))
    for _ in range(Z // 2 - 2):
        after, before = move(downs[-1], 0, 1, 0), move(ups[-1], 0, -1, 0)
        ups.append(after)
        downs.append(before)
    half = rows // 2
    opposite = [move(downs[-1][:half], 0, 1, 0), move(ups[-1][half:], 0, -1, 0)]
    held = {0: [blocks], -Z // 2: opposite}
    for step in range(1, Z // 2):
        held[step] = [ups[step]]
        held[-step] = [downs[step]]
    held[Z // 2] = opposite

    place = jnp.stack([y, z, core])
    got = []
    for near in CHUNKS:
        sources = [array for offset in near for array in held[offset]]
        own, swap, *sends = make_pick(near, rows, request, place, sources)
        arrived = [move(send, step + 1, 0, 0) for step, send in enumerate(sends)]
        swap = jnp.stack([swap] + [array[1] for array in arrived])
        got += [own] + arrived + [move(swap, 0, 0, 1)]
    return make_sum(where, used, bias[:, None], got).T


def solution(mesh):
    in_specs = (
        P("dom", "rep"),
        P("dom", None),
        P("rep", None),
        P("rep"),
        P("dom", None, None, None),
        P("dom", None),
        P("dom"),
    )
    out_specs = P("dom", "rep")
    return jax.shard_map(body, mesh=mesh, in_specs=in_specs, out_specs=out_specs, check_vma=False)
```

profile of v0, /device:TPU:1, one launch (start us, length us, event | category | flops | bytes accessed | tf_op | source)
XLA Modules:
  0.0 75.0 jit_solution(8212358585677508659)
XLA Ops:
  0.0 1.0 %pad_maximum_fusion.1.x0_ref = bf16[64,2304]{1,0:T(8,128)(2,1)S(1)} fusion(bf16[64,256]{1,0:T(8,128)(2,1)} %param.9, bf16[64,2048]{1,0:T(8,128)(2,1)} %bitcast.31), kind=kLoop, calls=%fused_computation.5 | loop fusion | flops 589824 | bytes 589824 | tf_op jit(solution)/shard_map/concatenate | solution.py:200
  1.0 2.1 %collective-permute-start = (bf16[64,2304]{1,0:T(8,128)(2,1)S(1)}, bf16[64,2304]{1,0:T(8,128)(2,1)S(1)}, u32[]{:S(2)}, u32[]{:S(2)}) collective-permute-start(bf16[64,2304]{1,0:T(8,128)(2,1)S(1)} %pad_maximum_fusion.1.x0_ref), channel_id=1, source_target_pairs={{0,1},{1,2},{2,3},{3,0},{4,5},{5,6},{6,7},{7,4},{8,9},{9,10},{10,1... | collective-permute-start | bytes 884744 | tf_op jit(solution)/shard_map/ppermute | solution.py:202
  3.1 2.5 %collective-permute-start.1 = (bf16[64,2304]{1,0:T(8,128)(2,1)S(1)}, bf16[64,2304]{1,0:T(8,128)(2,1)S(1)}, u32[]{:S(2)}, u32[]{:S(2)}) collective-permute-start(bf16[64,2304]{1,0:T(8,128)(2,1)S(1)} %pad_maximum_fusion.1.x0_ref), channel_id=1, source_target_pairs={{0,2},{1,3},{2,0},{3,1},{4,6},{5,7},{6,4},{7,5},{8,10},{9,11},{10,... | collective-permute-start | bytes 884744 | tf_op jit(solution)/shard_map/ppermute | solution.py:202
  5.6 1.2 %collective-permute-start.2 = (bf16[64,2304]{1,0:T(8,128)(2,1)S(1)}, bf16[64,2304]{1,0:T(8,128)(2,1)S(1)}, u32[]{:S(2)}, u32[]{:S(2)}) collective-permute-start(bf16[64,2304]{1,0:T(8,128)(2,1)S(1)} %pad_maximum_fusion.1.x0_ref), channel_id=1, source_target_pairs={{0,3},{1,0},{2,1},{3,2},{4,7},{5,4},{6,5},{7,6},{8,11},{9,8},{10,9... | collective-permute-start | bytes 884744 | tf_op jit(solution)/shard_map/ppermute | solution.py:202
  6.8 0.8 %copy.14 = s32[16,8]{1,0:T(8,128)S(1)} copy(s32[16,8]{0,1:T(8,128)} %param.12) | data formatting | bytes 1024 | tf_op args[5]
  7.7 0.5 fusion
  8.2 0.6 add_select_fusion
  8.9 6.0 %all-to-all-start = ((s32[8,1,128]{2,1,0:T(1,128)}), s32[8,1,128]{2,1,0:T(1,128)S(1)}, u32[]{:S(2)}, u32[]{:S(2)}) async-start(s32[8,1,128]{2,1,0:T(1,128)} %bitcast.3), calls=%async_computation | async-start | bytes 8192 | tf_op jit(solution)/shard_map/all_to_all | solution.py:222
  14.8 0.7 broadcast_and_fusion.order_ref
  15.5 3.9 %all-to-all-done = s32[8,1,128]{2,1,0:T(1,128)S(1)} async-done(((s32[8,1,128]{2,1,0:T(1,128)}), s32[8,1,128]{2,1,0:T(1,128)S(1)}, u32[]{:S(2)}, u32[]{:S(2)}) %all-to-all-start) | async-done | bytes 4128 | tf_op jit(solution)/shard_map/all_to_all | solution.py:222
  19.5 1.9 %hidden_blocks.1.refs_0_ = bf16[16,64,128]{2,1,0:T(8,128)(2,1)S(1)} custom-call(s32[1]{0:T(128)} %bitcast.rep_ref, s32[1,2048]{1,0:T(1,128)S(1)} %broadcast_and_fusion.order_ref, bf16[64,2304]{1,0:T(8,128)(2,1)S(1)} %pad_maximum_fusion.1.x0_ref, bf16[64,2304]{1,0:T(8,128)(2,1)S(1)} %collective-permute-done.x1_ref, ...), custom_call_target="tpu_custom_call" | custom-call | flops 400000000 | bytes 8000000 | tf_op jit(solution)/shard_map/hidden_blocks/pallas_call | solution.py:52
  21.4 1.7 %collective-permute-start.3 = (bf16[16,64,128]{2,1,0:T(8,128)(2,1)S(1)}, bf16[16,64,128]{2,1,0:T(8,128)(2,1)S(1)}, u32[]{:S(2)}, u32[]{:S(2)}) collective-permute-start(bf16[16,64,128]{2,1,0:T(8,128)(2,1)S(1)} %hidden_blocks.1.refs_0_), channel_id=1, source_target_pairs={{0,8},{4,12},{8,0},{12,4},{16,24},{20,28},{24,16},{28,20},{32,40},... | collective-permute-start | bytes 786440 | tf_op jit(solution)/shard_map/ppermute | solution.py:190
  23.1 4.7 %collective-permute-start.4 = (bf16[16,64,128]{2,1,0:T(8,128)(2,1)S(1)}, bf16[16,64,128]{2,1,0:T(8,128)(2,1)S(1)}, u32[]{:S(2)}, u32[]{:S(2)}) collective-permute-start(bf16[16,64,128]{2,1,0:T(8,128)(2,1)S(1)} %hidden_blocks.1.refs_0_), channel_id=1, source_target_pairs={{0,56},{4,60},{8,16},{12,20},{16,8},{20,12},{24,32},{28,36},{32,24... | collective-permute-start | bytes 786440 | tf_op jit(solution)/shard_map/ppermute | solution.py:190
  27.8 2.2 %copy-done.2 = bf16[16,8,128,128]{3,2,1,0:T(8,128)(2,1)S(1)} copy-done((bf16[16,8,128,128]{3,2,1,0:T(8,128)(2,1)S(1)}, bf16[16,8,128,128]{3,2,1,0:T(8,128)(2,1)}, u32[]{:S(2)}) %copy-start.2) | copy-done | bytes 4194328
  30.0 0.7 copy-done.3
  30.6 1.5 %load_tiles.1.tiles_ref = bf16[16,8,128,128]{3,2,1,0:T(8,128)(2,1)S(1)} custom-call(s32[16]{0:T(128)S(1)} %copy-done.3, bf16[16,8,128,128]{3,2,1,0:T(8,128)(2,1)S(1)} %copy-done.2), custom_call_target="tpu_custom_call" | custom-call | bytes 8000000 | tf_op jit(solution)/shard_map/load_tiles/pallas_call | solution.py:165
  32.2 2.0 %copy-done = bf16[16,8,128,128]{3,2,1,0:T(8,128)(2,1)} copy-done((bf16[16,8,128,128]{3,2,1,0:T(8,128)(2,1)}, bf16[16,8,128,128]{3,2,1,0:T(8,128)(2,1)S(1)}, u32[]{:S(2)}) %copy-start) | copy-done | bytes 4194328
  34.1 1.8 %collective-permute-start.9 = (bf16[16,64,128]{2,1,0:T(8,128)(2,1)S(1)}, bf16[16,64,128]{2,1,0:T(8,128)(2,1)S(1)}, u32[]{:S(2)}, u32[]{:S(2)}) collective-permute-start(bf16[16,64,128]{2,1,0:T(8,128)(2,1)S(1)} %collective-permute-done.3.refs_0_), channel_id=1, source_target_pairs={{0,56},{4,60},{8,16},{12,20},{16,8},{20,12},{24,32},{28,36},{32,24... | collective-permute-start | bytes 786440 | tf_op jit(solution)/shard_map/ppermute | solution.py:190
  36.0 0.7 pick_blocks.4
  36.7 0.2 collective-permute-start.5
  36.9 2.3 %collective-permute-start.6 = (bf16[2,2,2,64,128]{4,3,2,1,0:T(8,128)(2,1)S(1)}, bf16[2,2,2,64,128]{4,3,2,1,0:T(8,128)(2,1)S(1)}, u32[]{:S(2)}, u32[]{:S(2)}) collective-permute-start(bf16[2,2,2,64,128]{4,3,2,1,0:T(8,128)(2,1)S(1)} %get-tuple-element.44), channel_id=1, source_target_pairs={{0,128},{4,132},{8,136},{12,140},{16,144},{20,148},{24,152},{28,15... | collective-permute-start | bytes 393224 | tf_op jit(solution)/shard_map/ppermute | solution.py:190
  39.2 1.1 %collective-permute-start.7 = (bf16[2,2,2,64,128]{4,3,2,1,0:T(8,128)(2,1)S(1)}, bf16[2,2,2,64,128]{4,3,2,1,0:T(8,128)(2,1)S(1)}, u32[]{:S(2)}, u32[]{:S(2)}) collective-permute-start(bf16[2,2,2,64,128]{4,3,2,1,0:T(8,128)(2,1)S(1)} %get-tuple-element.45), channel_id=1, source_target_pairs={{0,192},{4,196},{8,200},{12,204},{16,208},{20,212},{24,216},{28,22... | collective-permute-start | bytes 393224 | tf_op jit(solution)/shard_map/ppermute | solution.py:190
  40.3 0.5 collective-permute-done.10.refs_2_
  40.8 1.2 %collective-permute-start.15 = (bf16[16,64,128]{2,1,0:T(8,128)(2,1)S(1)}, bf16[16,64,128]{2,1,0:T(8,128)(2,1)S(1)}, u32[]{:S(2)}, u32[]{:S(2)}) collective-permute-start(bf16[16,64,128]{2,1,0:T(8,128)(2,1)S(1)} %collective-permute-done.10.refs_2_), channel_id=1, source_target_pairs={{0,56},{4,60},{8,16},{12,20},{16,8},{20,12},{24,32},{28,36},{32,24... | collective-permute-start | bytes 786440 | tf_op jit(solution)/shard_map/ppermute | solution.py:190
  42.0 0.1 collective-permute-done.9.refs_1_
  42.1 0.8 %pick_blocks.5 = (bf16[3,2,64,128]{3,2,1,0:T(8,128)(2,1)S(1)}, bf16[3,2,64,128]{3,2,1,0:T(8,128)(2,1)S(1)}, bf16[2,3,2,64,128]{4,3,2,1,0:T(8,128)(2,1)S(1)}, bf1...) custom-call(s32[8,128]{1,0:T(8,128)S(1)} %bitcast.24, s32[3]{0:T(128)S(1)} %pad_add_fusion.place_ref, ...), custom_call_target="tpu_custom_call" | custom-call | tf_op jit(solution)/shard_map/pick_blocks/pallas_call | solution.py:96
  42.9 0.8 %collective-permute-done.5.refs_1_ = bf16[2,2,2,64,128]{4,3,2,1,0:T(8,128)(2,1)S(1)} collective-permute-done((bf16[2,2,2,64,128]{4,3,2,1,0:T(8,128)(2,1)S(1)}, bf16[2,2,2,64,128]{4,3,2,1,0:T(8,128)(2,1)S(1)}, u32[]{:S(2)}, u32[]{:S(2)}) %collective-permute-start.5) | collective-permute-done | bytes 131104 | tf_op jit(solution)/shard_map/ppermute | solution.py:190
  43.7 1.8 %collective-permute-start.12 = (bf16[2,3,2,64,128]{4,3,2,1,0:T(8,128)(2,1)S(1)}, bf16[2,3,2,64,128]{4,3,2,1,0:T(8,128)(2,1)S(1)}, u32[]{:S(2)}, u32[]{:S(2)}) collective-permute-start(bf16[2,3,2,64,128]{4,3,2,1,0:T(8,128)(2,1)S(1)} %get-tuple-element.50), channel_id=1, source_target_pairs={{0,128},{4,132},{8,136},{12,140},{16,144},{20,148},{24,152},{28,15... | collective-permute-start | bytes 589832 | tf_op jit(solution)/shard_map/ppermute | solution.py:190
  45.5 1.1 %collective-permute-start.13 = (bf16[2,3,2,64,128]{4,3,2,1,0:T(8,128)(2,1)S(1)}, bf16[2,3,2,64,128]{4,3,2,1,0:T(8,128)(2,1)S(1)}, u32[]{:S(2)}, u32[]{:S(2)}) collective-permute-start(bf16[2,3,2,64,128]{4,3,2,1,0:T(8,128)(2,1)S(1)} %get-tuple-element.51), channel_id=1, source_target_pairs={{0,192},{4,196},{8,200},{12,204},{16,208},{20,212},{24,216},{28,22... | collective-permute-start | bytes 589832 | tf_op jit(solution)/shard_map/ppermute | solution.py:190
  46.6 0.1 copy.16.bias_ref
  46.7 0.2 fusion.3
  47.0 0.3 collective-permute-done.15.refs_0_
  47.2 0.6 collective-permute-start.21
  47.8 1.7 %collective-permute-start.22 = (bf16[8,64,128]{2,1,0:T(8,128)(2,1)S(1)}, bf16[8,64,128]{2,1,0:T(8,128)(2,1)S(1)}, u32[]{:S(2)}, u32[]{:S(2)}) collective-permute-start(bf16[8,64,128]{2,1,0:T(8,128)(2,1)S(1)} %slice.66), channel_id=1, source_target_pairs={{0,56},{4,60},{8,16},{12,20},{16,8},{20,12},{24,32},{28,36},{32,24... | collective-permute-start | bytes 393224 | tf_op jit(solution)/shard_map/ppermute | solution.py:190
  49.5 0.7 pick_blocks.6
  50.2 2.3 %collective-permute-done.11.refs_6_ = bf16[2,3,2,64,128]{4,3,2,1,0:T(8,128)(2,1)S(1)} collective-permute-done((bf16[2,3,2,64,128]{4,3,2,1,0:T(8,128)(2,1)S(1)}, bf16[2,3,2,64,128]{4,3,2,1,0:T(8,128)(2,1)S(1)}, u32[]{:S(2)}, u32[]{:S(2)}) %collective-permute-start.11) | collective-permute-done | bytes 196640 | tf_op jit(solution)/shard_map/ppermute | solution.py:190
  52.5 0.4 collective-permute-start.18
  53.0 2.3 %collective-permute-start.19 = (bf16[2,2,2,64,128]{4,3,2,1,0:T(8,128)(2,1)S(1)}, bf16[2,2,2,64,128]{4,3,2,1,0:T(8,128)(2,1)S(1)}, u32[]{:S(2)}, u32[]{:S(2)}) collective-permute-start(bf16[2,2,2,64,128]{4,3,2,1,0:T(8,128)(2,1)S(1)} %get-tuple-element.56), channel_id=1, source_target_pairs={{0,192},{4,196},{8,200},{12,204},{16,208},{20,212},{24,216},{28,22... | collective-permute-start | bytes 393224 | tf_op jit(solution)/shard_map/ppermute | solution.py:190
  55.5 4.8 %collective-permute-start.8 = (bf16[4,2,2,64,128]{4,3,2,1,0:T(8,128)(2,1)S(1)}, bf16[4,2,2,64,128]{4,3,2,1,0:T(8,128)(2,1)S(1)}, u32[]{:S(2)}, u32[]{:S(2)}) collective-permute-start(bf16[4,2,2,64,128]{4,3,2,1,0:T(8,128)(2,1)S(1)} %pad_maximum_fusion.2), channel_id=1, source_target_pairs={{0,4},{4,0},{8,12},{12,8},{16,20},{20,16},{24,28},{28,24},{32,36},... | collective-permute-start | bytes 786440 | tf_op jit(solution)/shard_map/ppermute | solution.py:190
  60.3 0.1 collective-permute-start.14
  60.4 0.7 pick_blocks.7
  61.1 0.6 collective-permute-start.23
  61.7 1.7 %collective-permute-start.24 = (bf16[2,1,2,64,128]{4,3,2,1,0:T(8,128)(2,1)S(1)}, bf16[2,1,2,64,128]{4,3,2,1,0:T(8,128)(2,1)S(1)}, u32[]{:S(2)}, u32[]{:S(2)}) collective-permute-start(bf16[2,1,2,64,128]{4,3,2,1,0:T(8,128)(2,1)S(1)} %get-tuple-element.60), channel_id=1, source_target_pairs={{0,128},{4,132},{8,136},{12,140},{16,144},{20,148},{24,152},{28,15... | collective-permute-start | bytes 196616 | tf_op jit(solution)/shard_map/ppermute | solution.py:190
  63.4 2.1 %collective-permute-start.25 = (bf16[2,1,2,64,128]{4,3,2,1,0:T(8,128)(2,1)S(1)}, bf16[2,1,2,64,128]{4,3,2,1,0:T(8,128)(2,1)S(1)}, u32[]{:S(2)}, u32[]{:S(2)}) collective-permute-start(bf16[2,1,2,64,128]{4,3,2,1,0:T(8,128)(2,1)S(1)} %get-tuple-element.61), channel_id=1, source_target_pairs={{0,192},{4,196},{8,200},{12,204},{16,208},{20,212},{24,216},{28,22... | collective-permute-start | bytes 196616 | tf_op jit(solution)/shard_map/ppermute | solution.py:190
  65.6 4.4 %collective-permute-start.20 = (bf16[4,2,2,64,128]{4,3,2,1,0:T(8,128)(2,1)S(1)}, bf16[4,2,2,64,128]{4,3,2,1,0:T(8,128)(2,1)S(1)}, u32[]{:S(2)}, u32[]{:S(2)}) collective-permute-start(bf16[4,2,2,64,128]{4,3,2,1,0:T(8,128)(2,1)S(1)} %pad_maximum_fusion.3), channel_id=1, source_target_pairs={{0,4},{4,0},{8,12},{12,8},{16,20},{20,16},{24,28},{28,24},{32,36},... | collective-permute-start | bytes 786440 | tf_op jit(solution)/shard_map/ppermute | solution.py:190
  70.1 1.0 %collective-permute-start.26 = (bf16[4,1,2,64,128]{4,3,2,1,0:T(8,128)(2,1)S(1)}, bf16[4,1,2,64,128]{4,3,2,1,0:T(8,128)(2,1)S(1)}, u32[]{:S(2)}, u32[]{:S(2)}) collective-permute-start(bf16[4,1,2,64,128]{4,3,2,1,0:T(8,128)(2,1)S(1)} %pad_maximum_fusion.4), channel_id=1, source_target_pairs={{0,4},{4,0},{8,12},{12,8},{16,20},{20,16},{24,28},{28,24},{32,36},... | collective-permute-start | bytes 393224 | tf_op jit(solution)/shard_map/ppermute | solution.py:190
  71.1 0.9 %collective-permute-done.26.refs_19_ = bf16[4,1,2,64,128]{4,3,2,1,0:T(8,128)(2,1)S(1)} collective-permute-done((bf16[4,1,2,64,128]{4,3,2,1,0:T(8,128)(2,1)S(1)}, bf16[4,1,2,64,128]{4,3,2,1,0:T(8,128)(2,1)S(1)}, u32[]{:S(2)}, u32[]{:S(2)}) %collective-permute-start.26) | collective-permute-done | bytes 131104 | tf_op jit(solution)/shard_map/ppermute | solution.py:190
  72.1 3.0 %sum_tiles.1 = bf16[64,2048]{1,0:T(8,128)(2,1)} custom-call(s32[128]{0:T(128)S(1)} %convert_add_fusion.where_ref, bf16[16,8,128,128]{3,2,1,0:T(8,128)(2,1)S(1)} %copy-done.1, f32[64,1]{1,0:T(8,128)S(1)} %copy.16.bias_ref, bf16[2,2,64,128]{3,2,1,0:T(8,128)(2,1)S(1)} %get-tuple-element.42.refs_0_, ...), custom_call_target="tpu_custom_call" | custom-call | tf_op jit(solution)/shard_map/sum_tiles/pallas_call | solution.py:141
  (62 shorter events, 0.6 us)
Async XLA Ops:
  1.0 18.5 %collective-permute-start = (bf16[64,2304]{1,0:T(8,128)(2,1)S(1)}, bf16[64,2304]{1,0:T(8,128)(2,1)S(1)}, u32[]{:S(2)}, u32[]{:S(2)}) collective-permute-start(bf16[64,2304]{1,0:T(8,128)(2,1)S(1)} %pad_maximum_fusion.1.x0_ref), channel_id=1, source_target_pairs={{0,1},{1,2},{2,3},{3,0},{4,5},{5,6},{6,7},{7,4},{8,9},{9,10},{10,1... | collective-permute-start | bytes 884744 | tf_op jit(solution)/shard_map/ppermute | solution.py:202
  3.1 16.3 %collective-permute-start.1 = (bf16[64,2304]{1,0:T(8,128)(2,1)S(1)}, bf16[64,2304]{1,0:T(8,128)(2,1)S(1)}, u32[]{:S(2)}, u32[]{:S(2)}) collective-permute-start(bf16[64,2304]{1,0:T(8,128)(2,1)S(1)} %pad_maximum_fusion.1.x0_ref), channel_id=1, source_target_pairs={{0,2},{1,3},{2,0},{3,1},{4,6},{5,7},{6,4},{7,5},{8,10},{9,11},{10,... | collective-permute-start | bytes 884744 | tf_op jit(solution)/shard_map/ppermute | solution.py:202
  5.6 13.9 %collective-permute-start.2 = (bf16[64,2304]{1,0:T(8,128)(2,1)S(1)}, bf16[64,2304]{1,0:T(8,128)(2,1)S(1)}, u32[]{:S(2)}, u32[]{:S(2)}) collective-permute-start(bf16[64,2304]{1,0:T(8,128)(2,1)S(1)} %pad_maximum_fusion.1.x0_ref), channel_id=1, source_target_pairs={{0,3},{1,0},{2,1},{3,2},{4,7},{5,4},{6,5},{7,6},{8,11},{9,8},{10,9... | collective-permute-start | bytes 884744 | tf_op jit(solution)/shard_map/ppermute | solution.py:202
  8.9 10.6 %all-to-all-start = ((s32[8,1,128]{2,1,0:T(1,128)}), s32[8,1,128]{2,1,0:T(1,128)S(1)}, u32[]{:S(2)}, u32[]{:S(2)}) async-start(s32[8,1,128]{2,1,0:T(1,128)} %bitcast.3), calls=%async_computation | async-start | bytes 8192 | tf_op jit(solution)/shard_map/all_to_all | solution.py:222
  19.5 27.2 %copy-start.4 = (f32[64]{0:T(128)S(1)}, f32[64]{0:T(128)}, u32[]{:S(2)}) copy-start(f32[64]{0:T(128)} %param.10) | copy-start | bytes 772
  21.4 12.7 %collective-permute-start.3 = (bf16[16,64,128]{2,1,0:T(8,128)(2,1)S(1)}, bf16[16,64,128]{2,1,0:T(8,128)(2,1)S(1)}, u32[]{:S(2)}, u32[]{:S(2)}) collective-permute-start(bf16[16,64,128]{2,1,0:T(8,128)(2,1)S(1)} %hidden_blocks.1.refs_0_), channel_id=1, source_target_pairs={{0,8},{4,12},{8,0},{12,4},{16,24},{20,28},{24,16},{28,20},{32,40},... | collective-permute-start | bytes 786440 | tf_op jit(solution)/shard_map/ppermute | solution.py:190
  23.1 11.0 %collective-permute-start.4 = (bf16[16,64,128]{2,1,0:T(8,128)(2,1)S(1)}, bf16[16,64,128]{2,1,0:T(8,128)(2,1)S(1)}, u32[]{:S(2)}, u32[]{:S(2)}) collective-permute-start(bf16[16,64,128]{2,1,0:T(8,128)(2,1)S(1)} %hidden_blocks.1.refs_0_), channel_id=1, source_target_pairs={{0,56},{4,60},{8,16},{12,20},{16,8},{20,12},{24,32},{28,36},{32,24... | collective-permute-start | bytes 786440 | tf_op jit(solution)/shard_map/ppermute | solution.py:190
  27.8 2.2 %copy-start.2 = (bf16[16,8,128,128]{3,2,1,0:T(8,128)(2,1)S(1)}, bf16[16,8,128,128]{3,2,1,0:T(8,128)(2,1)}, u32[]{:S(2)}) copy-start(bf16[16,8,128,128]{3,2,1,0:T(8,128)(2,1)} %tiles_ref.1) | copy-start | bytes 12582916
  30.0 0.7 copy-start.3
  32.2 2.0 %copy-start = (bf16[16,8,128,128]{3,2,1,0:T(8,128)(2,1)}, bf16[16,8,128,128]{3,2,1,0:T(8,128)(2,1)S(1)}, u32[]{:S(2)}) copy-start(bf16[16,8,128,128]{3,2,1,0:T(8,128)(2,1)S(1)} %load_tiles.1.tiles_ref) | copy-start | bytes 12582916
  34.1 6.7 %collective-permute-start.10 = (bf16[16,64,128]{2,1,0:T(8,128)(2,1)S(1)}, bf16[16,64,128]{2,1,0:T(8,128)(2,1)S(1)}, u32[]{:S(2)}, u32[]{:S(2)}) collective-permute-start(bf16[16,64,128]{2,1,0:T(8,128)(2,1)S(1)} %collective-permute-done.4.refs_1_), channel_id=1, source_target_pairs={{0,8},{4,12},{8,0},{12,4},{16,24},{20,28},{24,16},{28,20},{32,40},... | collective-permute-start | bytes 786440 | tf_op jit(solution)/shard_map/ppermute | solution.py:190
  34.1 8.0 %collective-permute-start.9 = (bf16[16,64,128]{2,1,0:T(8,128)(2,1)S(1)}, bf16[16,64,128]{2,1,0:T(8,128)(2,1)S(1)}, u32[]{:S(2)}, u32[]{:S(2)}) collective-permute-start(bf16[16,64,128]{2,1,0:T(8,128)(2,1)S(1)} %collective-permute-done.3.refs_0_), channel_id=1, source_target_pairs={{0,56},{4,60},{8,16},{12,20},{16,8},{20,12},{24,32},{28,36},{32,24... | collective-permute-start | bytes 786440 | tf_op jit(solution)/shard_map/ppermute | solution.py:190
  36.7 6.9 %collective-permute-start.5 = (bf16[2,2,2,64,128]{4,3,2,1,0:T(8,128)(2,1)S(1)}, bf16[2,2,2,64,128]{4,3,2,1,0:T(8,128)(2,1)S(1)}, u32[]{:S(2)}, u32[]{:S(2)}) collective-permute-start(bf16[2,2,2,64,128]{4,3,2,1,0:T(8,128)(2,1)S(1)} %get-tuple-element.43), channel_id=1, source_target_pairs={{0,64},{4,68},{8,72},{12,76},{16,80},{20,84},{24,88},{28,92},{32,9... | collective-permute-start | bytes 393224 | tf_op jit(solution)/shard_map/ppermute | solution.py:190
  36.9 6.8 %collective-permute-start.6 = (bf16[2,2,2,64,128]{4,3,2,1,0:T(8,128)(2,1)S(1)}, bf16[2,2,2,64,128]{4,3,2,1,0:T(8,128)(2,1)S(1)}, u32[]{:S(2)}, u32[]{:S(2)}) collective-permute-start(bf16[2,2,2,64,128]{4,3,2,1,0:T(8,128)(2,1)S(1)} %get-tuple-element.44), channel_id=1, source_target_pairs={{0,128},{4,132},{8,136},{12,140},{16,144},{20,148},{24,152},{28,15... | collective-permute-start | bytes 393224 | tf_op jit(solution)/shard_map/ppermute | solution.py:190
  39.2 6.3 %collective-permute-start.7 = (bf16[2,2,2,64,128]{4,3,2,1,0:T(8,128)(2,1)S(1)}, bf16[2,2,2,64,128]{4,3,2,1,0:T(8,128)(2,1)S(1)}, u32[]{:S(2)}, u32[]{:S(2)}) collective-permute-start(bf16[2,2,2,64,128]{4,3,2,1,0:T(8,128)(2,1)S(1)} %get-tuple-element.45), channel_id=1, source_target_pairs={{0,192},{4,196},{8,200},{12,204},{16,208},{20,212},{24,216},{28,22... | collective-permute-start | bytes 393224 | tf_op jit(solution)/shard_map/ppermute | solution.py:190
  40.8 6.4 %collective-permute-start.15 = (bf16[16,64,128]{2,1,0:T(8,128)(2,1)S(1)}, bf16[16,64,128]{2,1,0:T(8,128)(2,1)S(1)}, u32[]{:S(2)}, u32[]{:S(2)}) collective-permute-start(bf16[16,64,128]{2,1,0:T(8,128)(2,1)S(1)} %collective-permute-done.10.refs_2_), channel_id=1, source_target_pairs={{0,56},{4,60},{8,16},{12,20},{16,8},{20,12},{24,32},{28,36},{32,24... | collective-permute-start | bytes 786440 | tf_op jit(solution)/shard_map/ppermute | solution.py:190
  42.1 5.7 %collective-permute-start.16 = (bf16[16,64,128]{2,1,0:T(8,128)(2,1)S(1)}, bf16[16,64,128]{2,1,0:T(8,128)(2,1)S(1)}, u32[]{:S(2)}, u32[]{:S(2)}) collective-permute-start(bf16[16,64,128]{2,1,0:T(8,128)(2,1)S(1)} %collective-permute-done.9.refs_1_), channel_id=1, source_target_pairs={{0,8},{4,12},{8,0},{12,4},{16,24},{20,28},{24,16},{28,20},{32,40},... | collective-permute-start | bytes 786440 | tf_op jit(solution)/shard_map/ppermute | solution.py:190
  43.7 8.8 %collective-permute-start.11 = (bf16[2,3,2,64,128]{4,3,2,1,0:T(8,128)(2,1)S(1)}, bf16[2,3,2,64,128]{4,3,2,1,0:T(8,128)(2,1)S(1)}, u32[]{:S(2)}, u32[]{:S(2)}) collective-permute-start(bf16[2,3,2,64,128]{4,3,2,1,0:T(8,128)(2,1)S(1)} %get-tuple-element.49), channel_id=1, source_target_pairs={{0,64},{4,68},{8,72},{12,76},{16,80},{20,84},{24,88},{28,92},{32,9... | collective-permute-start | bytes 589832 | tf_op jit(solution)/shard_map/ppermute | solution.py:190
  43.7 8.8 %collective-permute-start.12 = (bf16[2,3,2,64,128]{4,3,2,1,0:T(8,128)(2,1)S(1)}, bf16[2,3,2,64,128]{4,3,2,1,0:T(8,128)(2,1)S(1)}, u32[]{:S(2)}, u32[]{:S(2)}) collective-permute-start(bf16[2,3,2,64,128]{4,3,2,1,0:T(8,128)(2,1)S(1)} %get-tuple-element.50), channel_id=1, source_target_pairs={{0,128},{4,132},{8,136},{12,140},{16,144},{20,148},{24,152},{28,15... | collective-permute-start | bytes 589832 | tf_op jit(solution)/shard_map/ppermute | solution.py:190
  45.5 7.5 %collective-permute-start.13 = (bf16[2,3,2,64,128]{4,3,2,1,0:T(8,128)(2,1)S(1)}, bf16[2,3,2,64,128]{4,3,2,1,0:T(8,128)(2,1)S(1)}, u32[]{:S(2)}, u32[]{:S(2)}) collective-permute-start(bf16[2,3,2,64,128]{4,3,2,1,0:T(8,128)(2,1)S(1)} %get-tuple-element.51), channel_id=1, source_target_pairs={{0,192},{4,196},{8,200},{12,204},{16,208},{20,212},{24,216},{28,22... | collective-permute-start | bytes 589832 | tf_op jit(solution)/shard_map/ppermute | solution.py:190
  46.7 25.3 %copy-start.1 = (bf16[16,8,128,128]{3,2,1,0:T(8,128)(2,1)S(1)}, bf16[16,8,128,128]{3,2,1,0:T(8,128)(2,1)}, u32[]{:S(2)}) copy-start(bf16[16,8,128,128]{3,2,1,0:T(8,128)(2,1)} %copy-done) | copy-start | bytes 12582916
  47.2 8.2 %collective-permute-start.21 = (bf16[8,64,128]{2,1,0:T(8,128)(2,1)S(1)}, bf16[8,64,128]{2,1,0:T(8,128)(2,1)S(1)}, u32[]{:S(2)}, u32[]{:S(2)}) collective-permute-start(bf16[8,64,128]{2,1,0:T(8,128)(2,1)S(1)} %slice.65), channel_id=1, source_target_pairs={{0,8},{4,12},{8,0},{12,4},{16,24},{20,28},{24,16},{28,20},{32,40},... | collective-permute-start | bytes 393224 | tf_op jit(solution)/shard_map/ppermute | solution.py:190
  47.8 12.5 %collective-permute-start.22 = (bf16[8,64,128]{2,1,0:T(8,128)(2,1)S(1)}, bf16[8,64,128]{2,1,0:T(8,128)(2,1)S(1)}, u32[]{:S(2)}, u32[]{:S(2)}) collective-permute-start(bf16[8,64,128]{2,1,0:T(8,128)(2,1)S(1)} %slice.66), channel_id=1, source_target_pairs={{0,56},{4,60},{8,16},{12,20},{16,8},{20,12},{24,32},{28,36},{32,24... | collective-permute-start | bytes 393224 | tf_op jit(solution)/shard_map/ppermute | solution.py:190
  52.5 8.6 %collective-permute-start.17 = (bf16[2,2,2,64,128]{4,3,2,1,0:T(8,128)(2,1)S(1)}, bf16[2,2,2,64,128]{4,3,2,1,0:T(8,128)(2,1)S(1)}, u32[]{:S(2)}, u32[]{:S(2)}) collective-permute-start(bf16[2,2,2,64,128]{4,3,2,1,0:T(8,128)(2,1)S(1)} %get-tuple-element.54), channel_id=1, source_target_pairs={{0,64},{4,68},{8,72},{12,76},{16,80},{20,84},{24,88},{28,92},{32,9... | collective-permute-start | bytes 393224 | tf_op jit(solution)/shard_map/ppermute | solution.py:190
  52.5 9.2 %collective-permute-start.18 = (bf16[2,2,2,64,128]{4,3,2,1,0:T(8,128)(2,1)S(1)}, bf16[2,2,2,64,128]{4,3,2,1,0:T(8,128)(2,1)S(1)}, u32[]{:S(2)}, u32[]{:S(2)}) collective-permute-start(bf16[2,2,2,64,128]{4,3,2,1,0:T(8,128)(2,1)S(1)} %get-tuple-element.55), channel_id=1, source_target_pairs={{0,128},{4,132},{8,136},{12,140},{16,144},{20,148},{24,152},{28,15... | collective-permute-start | bytes 393224 | tf_op jit(solution)/shard_map/ppermute | solution.py:190
  53.0 10.4 %collective-permute-start.19 = (bf16[2,2,2,64,128]{4,3,2,1,0:T(8,128)(2,1)S(1)}, bf16[2,2,2,64,128]{4,3,2,1,0:T(8,128)(2,1)S(1)}, u32[]{:S(2)}, u32[]{:S(2)}) collective-permute-start(bf16[2,2,2,64,128]{4,3,2,1,0:T(8,128)(2,1)S(1)} %get-tuple-element.56), channel_id=1, source_target_pairs={{0,192},{4,196},{8,200},{12,204},{16,208},{20,212},{24,216},{28,22... | collective-permute-start | bytes 393224 | tf_op jit(solution)/shard_map/ppermute | solution.py:190
  55.5 15.6 %collective-permute-start.8 = (bf16[4,2,2,64,128]{4,3,2,1,0:T(8,128)(2,1)S(1)}, bf16[4,2,2,64,128]{4,3,2,1,0:T(8,128)(2,1)S(1)}, u32[]{:S(2)}, u32[]{:S(2)}) collective-permute-start(bf16[4,2,2,64,128]{4,3,2,1,0:T(8,128)(2,1)S(1)} %pad_maximum_fusion.2), channel_id=1, source_target_pairs={{0,4},{4,0},{8,12},{12,8},{16,20},{20,16},{24,28},{28,24},{32,36},... | collective-permute-start | bytes 786440 | tf_op jit(solution)/shard_map/ppermute | solution.py:190
  60.3 11.8 %collective-permute-start.14 = (bf16[4,3,2,64,128]{4,3,2,1,0:T(8,128)(2,1)S(1)}, bf16[4,3,2,64,128]{4,3,2,1,0:T(8,128)(2,1)S(1)}, u32[]{:S(2)}, u32[]{:S(2)}) collective-permute-start(bf16[4,3,2,64,128]{4,3,2,1,0:T(8,128)(2,1)S(1)} %pad_maximum_fusion), channel_id=1, source_target_pairs={{0,4},{4,0},{8,12},{12,8},{16,20},{20,16},{24,28},{28,24},{32,36},... | collective-permute-start | bytes 1179656 | tf_op jit(solution)/shard_map/ppermute | solution.py:190
  61.1 4.5 %collective-permute-start.23 = (bf16[2,1,2,64,128]{4,3,2,1,0:T(8,128)(2,1)S(1)}, bf16[2,1,2,64,128]{4,3,2,1,0:T(8,128)(2,1)S(1)}, u32[]{:S(2)}, u32[]{:S(2)}) collective-permute-start(bf16[2,1,2,64,128]{4,3,2,1,0:T(8,128)(2,1)S(1)} %get-tuple-element.59), channel_id=1, source_target_pairs={{0,64},{4,68},{8,72},{12,76},{16,80},{20,84},{24,88},{28,92},{32,9... | collective-permute-start | bytes 196616 | tf_op jit(solution)/shard_map/ppermute | solution.py:190
  61.7 8.3 %collective-permute-start.24 = (bf16[2,1,2,64,128]{4,3,2,1,0:T(8,128)(2,1)S(1)}, bf16[2,1,2,64,128]{4,3,2,1,0:T(8,128)(2,1)S(1)}, u32[]{:S(2)}, u32[]{:S(2)}) collective-permute-start(bf16[2,1,2,64,128]{4,3,2,1,0:T(8,128)(2,1)S(1)} %get-tuple-element.60), channel_id=1, source_target_pairs={{0,128},{4,132},{8,136},{12,140},{16,144},{20,148},{24,152},{28,15... | collective-permute-start | bytes 196616 | tf_op jit(solution)/shard_map/ppermute | solution.py:190
  63.4 6.6 %collective-permute-start.25 = (bf16[2,1,2,64,128]{4,3,2,1,0:T(8,128)(2,1)S(1)}, bf16[2,1,2,64,128]{4,3,2,1,0:T(8,128)(2,1)S(1)}, u32[]{:S(2)}, u32[]{:S(2)}) collective-permute-start(bf16[2,1,2,64,128]{4,3,2,1,0:T(8,128)(2,1)S(1)} %get-tuple-element.61), channel_id=1, source_target_pairs={{0,192},{4,196},{8,200},{12,204},{16,208},{20,212},{24,216},{28,22... | collective-permute-start | bytes 196616 | tf_op jit(solution)/shard_map/ppermute | solution.py:190
  65.6 6.4 %collective-permute-start.20 = (bf16[4,2,2,64,128]{4,3,2,1,0:T(8,128)(2,1)S(1)}, bf16[4,2,2,64,128]{4,3,2,1,0:T(8,128)(2,1)S(1)}, u32[]{:S(2)}, u32[]{:S(2)}) collective-permute-start(bf16[4,2,2,64,128]{4,3,2,1,0:T(8,128)(2,1)S(1)} %pad_maximum_fusion.3), channel_id=1, source_target_pairs={{0,4},{4,0},{8,12},{12,8},{16,20},{20,16},{24,28},{28,24},{32,36},... | collective-permute-start | bytes 786440 | tf_op jit(solution)/shard_map/ppermute | solution.py:190
  70.1 2.0 %collective-permute-start.26 = (bf16[4,1,2,64,128]{4,3,2,1,0:T(8,128)(2,1)S(1)}, bf16[4,1,2,64,128]{4,3,2,1,0:T(8,128)(2,1)S(1)}, u32[]{:S(2)}, u32[]{:S(2)}) collective-permute-start(bf16[4,1,2,64,128]{4,3,2,1,0:T(8,128)(2,1)S(1)} %pad_maximum_fusion.4), channel_id=1, source_target_pairs={{0,4},{4,0},{8,12},{12,8},{16,20},{20,16},{24,28},{28,24},{32,36},... | collective-permute-start | bytes 393224 | tf_op jit(solution)/shard_map/ppermute | solution.py:190
where the time goes:
time: 75.3 us; the launch traced here: 75 us
  starting transfers between devices  47.3 us (63%)
  Pallas kernels  9.28 us (12%)
  waiting for transfers between devices  8.96 us (12%)
  local copies, waits for them, and re-layouts  5.84 us (8%)
  other arithmetic  3.36 us (4%)
    ppermute x24, starting transfers between devices, move(): return lax.ppermute(array, 'dom', pairs)  35.6 us
    all_to_all x1, starting transfers between devices, body(): lax.all_to_all(request, 'dom', 0, 0, axis_index_groups=groups, tiled=True)  5.98 us
    ppermute x3, starting transfers between devices, body(): lax.ppermute(mine, 'rep', [(i, (i + shift) % reps) for i in range(reps)])  5.72 us
    unnamed x11, local copies, waits for them, and re-layouts  5.57 us
    ppermute x24, waiting for transfers between devices, move(): return lax.ppermute(array, 'dom', pairs)  5.05 us
    all_to_all x1, waiting for transfers between devices, body(): lax.all_to_all(request, 'dom', 0, 0, axis_index_groups=groups, tiled=True)  3.91 us
    pallas_call x1, Pallas kernels, make_sum(): pl.pallas_call(sum_kernel, out_shape=jax.ShapeDtypeStruct((width, rows *...  2.95 us
    pallas_call x4, Pallas kernels, make_pick(): pl.pallas_call(functools.partial(pick_kernel, near, count), out_shape=(on...  2.88 us
  transfers between devices with their start and end apart: 28, of which 7 were waited for; matrix products, arithmetic and copies ran while one was open for 5% of the time, Pallas kernels for 6%

commit v1 on v0

--- a/solution.py
+++ b/solution.py
@@ -8,6 +8,7 @@
 from jax.sharding import PartitionSpec as P
 
 VMEM_LIMIT = 24 * 1024 * 1024
+LOAD_STEPS = 4
 VMEM = pl.BlockSpec(memory_space=pltpu.VMEM)
 SMEM = pl.BlockSpec(memory_space=pltpu.SMEM)
 Y, Z, CORES = 4, 8, 2
@@ -151,22 +152,23 @@
 
 def load_kernel(counts_ref, tiles_ref, used_ref):
     rows, slots = tiles_ref.shape[:2]
-
-    def load(row, carry):
+    first = pl.program_id(0) * rows
+    for row in range(rows):
+        used = counts_ref[first + row]
         for slot in range(slots):
             tile = tiles_ref[row, slot]
-            used_ref[row, slot] = jnp.where(slot < counts_ref[row], tile, jnp.zeros_like(tile))
-        return carry
-
-    lax.fori_loop(0, rows, load, 0, unroll=2)
+            used_ref[row, slot] = jnp.where(slot < used, tile, jnp.zeros_like(tile))
 
 
 def make_load(counts, tiles):
+    rows = tiles.shape[0] // LOAD_STEPS
+    block = pl.BlockSpec((rows,) + tiles.shape[1:], lambda index: (index, 0, 0, 0))
     return pl.pallas_call(
         load_kernel,
+        grid=(LOAD_STEPS,),
         out_shape=jax.ShapeDtypeStruct(tiles.shape, tiles.dtype),
-        in_specs=[SMEM, VMEM],
-        out_specs=VMEM,
+        in_specs=[SMEM, block],
+        out_specs=block,
         compiler_params=pltpu.CompilerParams(vmem_limit_bytes=VMEM_LIMIT),
         cost_estimate=pl.CostEstimate(flops=0, bytes_accessed=8_000_000, transcendentals=0),
         name="load_tiles",

time: 75.3 us -> 74.1 us (0.984)
  starting transfers between devices: 47.3 us -> 45.8 us
    ppermute x24, starting transfers between devices: 35.6 us -> 34.1 us  [move(): return lax.ppermute(array, 'dom', pairs)]
  transfers between devices with their start and end apart: 28 -> 28, of which waited for: 7 -> 8; matrix products, arithmetic and copies ran while one was open for 5% -> 5% of each run, Pallas kernels for 6% -> 6%
where the time goes in v1:
time: 74.1 us; the launch traced here: 73.9 us
  starting transfers between devices  45.8 us (62%)
  Pallas kernels  9.37 us (13%)
  waiting for transfers between devices  9.26 us (12%)
  local copies, waits for them, and re-layouts  5.84 us (8%)
  other arithmetic  3.36 us (5%)
    ppermute x24, starting transfers between devices, move(): return lax.ppermute(array, 'dom', pairs)  34.1 us
    all_to_all x1, starting transfers between devices, body(): lax.all_to_all(request, 'dom', 0, 0, axis_index_groups=groups, tiled=True)  5.98 us
    ppermute x3, starting transfers between devices, body(): lax.ppermute(mine, 'rep', [(i, (i + shift) % reps) for i in range(reps)])  5.72 us
    unnamed x11, local copies, waits for them, and re-layouts  5.57 us
    ppermute x24, waiting for transfers between devices, move(): return lax.ppermute(array, 'dom', pairs)  5.35 us
    all_to_all x1, waiting for transfers between devices, body(): lax.all_to_all(request, 'dom', 0, 0, axis_index_groups=groups, tiled=True)  3.91 us
    pallas_call x1, Pallas kernels, make_sum(): pl.pallas_call(sum_kernel, out_shape=jax.ShapeDtypeStruct((width, rows *...  2.95 us
    pallas_call x4, Pallas kernels, make_pick(): pl.pallas_call(functools.partial(pick_kernel, near, count), out_shape=(on...  2.88 us
  transfers between devices with their start and end apart: 28, of which 8 were waited for; matrix products, arithmetic and copies ran while one was open for 5% of the time, Pallas kernels for 6%

profile of v1, /device:TPU:1, one launch (start us, length us, event | category | flops | bytes accessed | tf_op | source)
XLA Modules:
  0.0 73.9 jit_solution(4393135086819093977)
XLA Ops:
  0.0 1.0 %pad_maximum_fusion.1.x0_ref = bf16[64,2304]{1,0:T(8,128)(2,1)S(1)} fusion(bf16[64,256]{1,0:T(8,128)(2,1)} %param.9, bf16[64,2048]{1,0:T(8,128)(2,1)} %bitcast.31), kind=kLoop, calls=%fused_computation.5 | loop fusion | flops 589824 | bytes 589824 | tf_op jit(solution)/shard_map/concatenate | solution.py:202
  1.0 2.1 %collective-permute-start = (bf16[64,2304]{1,0:T(8,128)(2,1)S(1)}, bf16[64,2304]{1,0:T(8,128)(2,1)S(1)}, u32[]{:S(2)}, u32[]{:S(2)}) collective-permute-start(bf16[64,2304]{1,0:T(8,128)(2,1)S(1)} %pad_maximum_fusion.1.x0_ref), channel_id=1, source_target_pairs={{0,1},{1,2},{2,3},{3,0},{4,5},{5,6},{6,7},{7,4},{8,9},{9,10},{10,1... | collective-permute-start | bytes 884744 | tf_op jit(solution)/shard_map/ppermute | solution.py:204
  3.1 2.5 %collective-permute-start.1 = (bf16[64,2304]{1,0:T(8,128)(2,1)S(1)}, bf16[64,2304]{1,0:T(8,128)(2,1)S(1)}, u32[]{:S(2)}, u32[]{:S(2)}) collective-permute-start(bf16[64,2304]{1,0:T(8,128)(2,1)S(1)} %pad_maximum_fusion.1.x0_ref), channel_id=1, source_target_pairs={{0,2},{1,3},{2,0},{3,1},{4,6},{5,7},{6,4},{7,5},{8,10},{9,11},{10,... | collective-permute-start | bytes 884744 | tf_op jit(solution)/shard_map/ppermute | solution.py:204
  5.6 1.2 %collective-permute-start.2 = (bf16[64,2304]{1,0:T(8,128)(2,1)S(1)}, bf16[64,2304]{1,0:T(8,128)(2,1)S(1)}, u32[]{:S(2)}, u32[]{:S(2)}) collective-permute-start(bf16[64,2304]{1,0:T(8,128)(2,1)S(1)} %pad_maximum_fusion.1.x0_ref), channel_id=1, source_target_pairs={{0,3},{1,0},{2,1},{3,2},{4,7},{5,4},{6,5},{7,6},{8,11},{9,8},{10,9... | collective-permute-start | bytes 884744 | tf_op jit(solution)/shard_map/ppermute | solution.py:204
  6.8 0.8 %copy.14 = s32[16,8]{1,0:T(8,128)S(1)} copy(s32[16,8]{0,1:T(8,128)} %param.12) | data formatting | bytes 1024 | tf_op args[5]
  7.7 0.5 fusion
  8.2 0.6 add_select_fusion
  8.9 6.0 %all-to-all-start = ((s32[8,1,128]{2,1,0:T(1,128)}), s32[8,1,128]{2,1,0:T(1,128)S(1)}, u32[]{:S(2)}, u32[]{:S(2)}) async-start(s32[8,1,128]{2,1,0:T(1,128)} %bitcast.3), calls=%async_computation | async-start | bytes 8192 | tf_op jit(solution)/shard_map/all_to_all | solution.py:224
  14.8 0.7 broadcast_and_fusion.order_ref
  15.5 3.9 %all-to-all-done = s32[8,1,128]{2,1,0:T(1,128)S(1)} async-done(((s32[8,1,128]{2,1,0:T(1,128)}), s32[8,1,128]{2,1,0:T(1,128)S(1)}, u32[]{:S(2)}, u32[]{:S(2)}) %all-to-all-start) | async-done | bytes 4128 | tf_op jit(solution)/shard_map/all_to_all | solution.py:224
  19.5 1.9 %hidden_blocks.1.refs_0_ = bf16[16,64,128]{2,1,0:T(8,128)(2,1)S(1)} custom-call(s32[1]{0:T(128)} %bitcast.rep_ref, s32[1,2048]{1,0:T(1,128)S(1)} %broadcast_and_fusion.order_ref, bf16[64,2304]{1,0:T(8,128)(2,1)S(1)} %pad_maximum_fusion.1.x0_ref, bf16[64,2304]{1,0:T(8,128)(2,1)S(1)} %collective-permute-done.x1_ref, ...), custom_call_target="tpu_custom_call" | custom-call | flops 400000000 | bytes 8000000 | tf_op jit(solution)/shard_map/hidden_blocks/pallas_call | solution.py:53
  21.4 1.7 %collective-permute-start.3 = (bf16[16,64,128]{2,1,0:T(8,128)(2,1)S(1)}, bf16[16,64,128]{2,1,0:T(8,128)(2,1)S(1)}, u32[]{:S(2)}, u32[]{:S(2)}) collective-permute-start(bf16[16,64,128]{2,1,0:T(8,128)(2,1)S(1)} %hidden_blocks.1.refs_0_), channel_id=1, source_target_pairs={{0,8},{4,12},{8,0},{12,4},{16,24},{20,28},{24,16},{28,20},{32,40},... | collective-permute-start | bytes 786440 | tf_op jit(solution)/shard_map/ppermute | solution.py:192
  23.1 4.7 %collective-permute-start.4 = (bf16[16,64,128]{2,1,0:T(8,128)(2,1)S(1)}, bf16[16,64,128]{2,1,0:T(8,128)(2,1)S(1)}, u32[]{:S(2)}, u32[]{:S(2)}) collective-permute-start(bf16[16,64,128]{2,1,0:T(8,128)(2,1)S(1)} %hidden_blocks.1.refs_0_), channel_id=1, source_target_pairs={{0,56},{4,60},{8,16},{12,20},{16,8},{20,12},{24,32},{28,36},{32,24... | collective-permute-start | bytes 786440 | tf_op jit(solution)/shard_map/ppermute | solution.py:192
  27.8 2.2 %copy-done.2 = bf16[16,8,128,128]{3,2,1,0:T(8,128)(2,1)S(1)} copy-done((bf16[16,8,128,128]{3,2,1,0:T(8,128)(2,1)S(1)}, bf16[16,8,128,128]{3,2,1,0:T(8,128)(2,1)}, u32[]{:S(2)}) %copy-start.2) | copy-done | bytes 4194328
  30.0 0.7 copy-done.3
  30.6 1.6 %load_tiles.1.tiles_ref = bf16[16,8,128,128]{3,2,1,0:T(8,128)(2,1)S(1)} custom-call(s32[16]{0:T(128)S(1)} %copy-done.3, bf16[16,8,128,128]{3,2,1,0:T(8,128)(2,1)S(1)} %copy-done.2), custom_call_target="tpu_custom_call" | custom-call | bytes 8000000 | tf_op jit(solution)/shard_map/load_tiles/pallas_call | solution.py:166
  32.3 2.0 %copy-done = bf16[16,8,128,128]{3,2,1,0:T(8,128)(2,1)} copy-done((bf16[16,8,128,128]{3,2,1,0:T(8,128)(2,1)}, bf16[16,8,128,128]{3,2,1,0:T(8,128)(2,1)S(1)}, u32[]{:S(2)}) %copy-start) | copy-done | bytes 4194328
  34.2 1.7 %collective-permute-start.9 = (bf16[16,64,128]{2,1,0:T(8,128)(2,1)S(1)}, bf16[16,64,128]{2,1,0:T(8,128)(2,1)S(1)}, u32[]{:S(2)}, u32[]{:S(2)}) collective-permute-start(bf16[16,64,128]{2,1,0:T(8,128)(2,1)S(1)} %collective-permute-done.3.refs_0_), channel_id=1, source_target_pairs={{0,56},{4,60},{8,16},{12,20},{16,8},{20,12},{24,32},{28,36},{32,24... | collective-permute-start | bytes 786440 | tf_op jit(solution)/shard_map/ppermute | solution.py:192
  36.0 0.7 pick_blocks.4
  36.7 0.3 collective-permute-start.5
  37.0 2.3 %collective-permute-start.6 = (bf16[2,2,2,64,128]{4,3,2,1,0:T(8,128)(2,1)S(1)}, bf16[2,2,2,64,128]{4,3,2,1,0:T(8,128)(2,1)S(1)}, u32[]{:S(2)}, u32[]{:S(2)}) collective-permute-start(bf16[2,2,2,64,128]{4,3,2,1,0:T(8,128)(2,1)S(1)} %get-tuple-element.44), channel_id=1, source_target_pairs={{0,128},{4,132},{8,136},{12,140},{16,144},{20,148},{24,152},{28,15... | collective-permute-start | bytes 393224 | tf_op jit(solution)/shard_map/ppermute | solution.py:192
  39.3 1.1 %collective-permute-start.7 = (bf16[2,2,2,64,128]{4,3,2,1,0:T(8,128)(2,1)S(1)}, bf16[2,2,2,64,128]{4,3,2,1,0:T(8,128)(2,1)S(1)}, u32[]{:S(2)}, u32[]{:S(2)}) collective-permute-start(bf16[2,2,2,64,128]{4,3,2,1,0:T(8,128)(2,1)S(1)} %get-tuple-element.45), channel_id=1, source_target_pairs={{0,192},{4,196},{8,200},{12,204},{16,208},{20,212},{24,216},{28,22... | collective-permute-start | bytes 393224 | tf_op jit(solution)/shard_map/ppermute | solution.py:192
  40.4 0.5 collective-permute-done.10.refs_2_
  40.9 1.1 %collective-permute-start.15 = (bf16[16,64,128]{2,1,0:T(8,128)(2,1)S(1)}, bf16[16,64,128]{2,1,0:T(8,128)(2,1)S(1)}, u32[]{:S(2)}, u32[]{:S(2)}) collective-permute-start(bf16[16,64,128]{2,1,0:T(8,128)(2,1)S(1)} %collective-permute-done.10.refs_2_), channel_id=1, source_target_pairs={{0,56},{4,60},{8,16},{12,20},{16,8},{20,12},{24,32},{28,36},{32,24... | collective-permute-start | bytes 786440 | tf_op jit(solution)/shard_map/ppermute | solution.py:192
  42.0 0.2 collective-permute-done.9.refs_1_
  42.2 0.8 %pick_blocks.5 = (bf16[3,2,64,128]{3,2,1,0:T(8,128)(2,1)S(1)}, bf16[3,2,64,128]{3,2,1,0:T(8,128)(2,1)S(1)}, bf16[2,3,2,64,128]{4,3,2,1,0:T(8,128)(2,1)S(1)}, bf1...) custom-call(s32[8,128]{1,0:T(8,128)S(1)} %bitcast.24, s32[3]{0:T(128)S(1)} %pad_add_fusion.place_ref, ...), custom_call_target="tpu_custom_call" | custom-call | tf_op jit(solution)/shard_map/pick_blocks/pallas_call | solution.py:97
  42.9 0.7 collective-permute-done.5.refs_1_
  43.6 2.0 %collective-permute-start.12 = (bf16[2,3,2,64,128]{4,3,2,1,0:T(8,128)(2,1)S(1)}, bf16[2,3,2,64,128]{4,3,2,1,0:T(8,128)(2,1)S(1)}, u32[]{:S(2)}, u32[]{:S(2)}) collective-permute-start(bf16[2,3,2,64,128]{4,3,2,1,0:T(8,128)(2,1)S(1)} %get-tuple-element.50), channel_id=1, source_target_pairs={{0,128},{4,132},{8,136},{12,140},{16,144},{20,148},{24,152},{28,15... | collective-permute-start | bytes 589832 | tf_op jit(solution)/shard_map/ppermute | solution.py:192
  45.6 1.0 %collective-permute-start.13 = (bf16[2,3,2,64,128]{4,3,2,1,0:T(8,128)(2,1)S(1)}, bf16[2,3,2,64,128]{4,3,2,1,0:T(8,128)(2,1)S(1)}, u32[]{:S(2)}, u32[]{:S(2)}) collective-permute-start(bf16[2,3,2,64,128]{4,3,2,1,0:T(8,128)(2,1)S(1)} %get-tuple-element.51), channel_id=1, source_target_pairs={{0,192},{4,196},{8,200},{12,204},{16,208},{20,212},{24,216},{28,22... | collective-permute-start | bytes 589832 | tf_op jit(solution)/shard_map/ppermute | solution.py:192
  46.7 0.2 fusion.3
  46.9 0.4 collective-permute-done.15.refs_0_
  47.3 0.6 collective-permute-start.21
  47.9 1.6 %collective-permute-start.22 = (bf16[8,64,128]{2,1,0:T(8,128)(2,1)S(1)}, bf16[8,64,128]{2,1,0:T(8,128)(2,1)S(1)}, u32[]{:S(2)}, u32[]{:S(2)}) collective-permute-start(bf16[8,64,128]{2,1,0:T(8,128)(2,1)S(1)} %slice.66), channel_id=1, source_target_pairs={{0,56},{4,60},{8,16},{12,20},{16,8},{20,12},{24,32},{28,36},{32,24... | collective-permute-start | bytes 393224 | tf_op jit(solution)/shard_map/ppermute | solution.py:192
  49.5 0.7 pick_blocks.6
  50.2 2.1 %collective-permute-done.11.refs_6_ = bf16[2,3,2,64,128]{4,3,2,1,0:T(8,128)(2,1)S(1)} collective-permute-done((bf16[2,3,2,64,128]{4,3,2,1,0:T(8,128)(2,1)S(1)}, bf16[2,3,2,64,128]{4,3,2,1,0:T(8,128)(2,1)S(1)}, u32[]{:S(2)}, u32[]{:S(2)}) %collective-permute-start.11) | collective-permute-done | bytes 196640 | tf_op jit(solution)/shard_map/ppermute | solution.py:192
  52.3 0.6 collective-permute-start.18
  52.9 2.2 %collective-permute-start.19 = (bf16[2,2,2,64,128]{4,3,2,1,0:T(8,128)(2,1)S(1)}, bf16[2,2,2,64,128]{4,3,2,1,0:T(8,128)(2,1)S(1)}, u32[]{:S(2)}, u32[]{:S(2)}) collective-permute-start(bf16[2,2,2,64,128]{4,3,2,1,0:T(8,128)(2,1)S(1)} %get-tuple-element.56), channel_id=1, source_target_pairs={{0,192},{4,196},{8,200},{12,204},{16,208},{20,212},{24,216},{28,22... | collective-permute-start | bytes 393224 | tf_op jit(solution)/shard_map/ppermute | solution.py:192
  55.2 5.2 %collective-permute-start.8 = (bf16[4,2,2,64,128]{4,3,2,1,0:T(8,128)(2,1)S(1)}, bf16[4,2,2,64,128]{4,3,2,1,0:T(8,128)(2,1)S(1)}, u32[]{:S(2)}, u32[]{:S(2)}) collective-permute-start(bf16[4,2,2,64,128]{4,3,2,1,0:T(8,128)(2,1)S(1)} %pad_maximum_fusion.2), channel_id=1, source_target_pairs={{0,4},{4,0},{8,12},{12,8},{16,20},{20,16},{24,28},{28,24},{32,36},... | collective-permute-start | bytes 786440 | tf_op jit(solution)/shard_map/ppermute | solution.py:192
  60.4 0.1 collective-permute-start.14
  60.5 0.7 pick_blocks.7
  61.2 0.7 collective-permute-start.23
  61.9 1.3 %collective-permute-start.24 = (bf16[2,1,2,64,128]{4,3,2,1,0:T(8,128)(2,1)S(1)}, bf16[2,1,2,64,128]{4,3,2,1,0:T(8,128)(2,1)S(1)}, u32[]{:S(2)}, u32[]{:S(2)}) collective-permute-start(bf16[2,1,2,64,128]{4,3,2,1,0:T(8,128)(2,1)S(1)} %get-tuple-element.60), channel_id=1, source_target_pairs={{0,128},{4,132},{8,136},{12,140},{16,144},{20,148},{24,152},{28,15... | collective-permute-start | bytes 196616 | tf_op jit(solution)/shard_map/ppermute | solution.py:192
  63.3 1.8 %collective-permute-start.25 = (bf16[2,1,2,64,128]{4,3,2,1,0:T(8,128)(2,1)S(1)}, bf16[2,1,2,64,128]{4,3,2,1,0:T(8,128)(2,1)S(1)}, u32[]{:S(2)}, u32[]{:S(2)}) collective-permute-start(bf16[2,1,2,64,128]{4,3,2,1,0:T(8,128)(2,1)S(1)} %get-tuple-element.61), channel_id=1, source_target_pairs={{0,192},{4,196},{8,200},{12,204},{16,208},{20,212},{24,216},{28,22... | collective-permute-start | bytes 196616 | tf_op jit(solution)/shard_map/ppermute | solution.py:192
  65.2 0.5 collective-permute-done.23.refs_16_
  65.6 2.4 %collective-permute-start.20 = (bf16[4,2,2,64,128]{4,3,2,1,0:T(8,128)(2,1)S(1)}, bf16[4,2,2,64,128]{4,3,2,1,0:T(8,128)(2,1)S(1)}, u32[]{:S(2)}, u32[]{:S(2)}) collective-permute-start(bf16[4,2,2,64,128]{4,3,2,1,0:T(8,128)(2,1)S(1)} %pad_maximum_fusion.3), channel_id=1, source_target_pairs={{0,4},{4,0},{8,12},{12,8},{16,20},{20,16},{24,28},{28,24},{32,36},... | collective-permute-start | bytes 786440 | tf_op jit(solution)/shard_map/ppermute | solution.py:192
  68.1 1.8 %collective-permute-start.26 = (bf16[4,1,2,64,128]{4,3,2,1,0:T(8,128)(2,1)S(1)}, bf16[4,1,2,64,128]{4,3,2,1,0:T(8,128)(2,1)S(1)}, u32[]{:S(2)}, u32[]{:S(2)}) collective-permute-start(bf16[4,1,2,64,128]{4,3,2,1,0:T(8,128)(2,1)S(1)} %pad_maximum_fusion.4), channel_id=1, source_target_pairs={{0,4},{4,0},{8,12},{12,8},{16,20},{20,16},{24,28},{28,24},{32,36},... | collective-permute-start | bytes 393224 | tf_op jit(solution)/shard_map/ppermute | solution.py:192
  70.0 0.9 %collective-permute-done.26.refs_19_ = bf16[4,1,2,64,128]{4,3,2,1,0:T(8,128)(2,1)S(1)} collective-permute-done((bf16[4,1,2,64,128]{4,3,2,1,0:T(8,128)(2,1)S(1)}, bf16[4,1,2,64,128]{4,3,2,1,0:T(8,128)(2,1)S(1)}, u32[]{:S(2)}, u32[]{:S(2)}) %collective-permute-start.26) | collective-permute-done | bytes 131104 | tf_op jit(solution)/shard_map/ppermute | solution.py:192
  70.9 3.0 %sum_tiles.1 = bf16[64,2048]{1,0:T(8,128)(2,1)} custom-call(s32[128]{0:T(128)S(1)} %convert_add_fusion.where_ref, bf16[16,8,128,128]{3,2,1,0:T(8,128)(2,1)S(1)} %copy-done.1, f32[64,1]{1,0:T(8,128)S(1)} %copy.16.bias_ref, bf16[2,2,64,128]{3,2,1,0:T(8,128)(2,1)S(1)} %get-tuple-element.42.refs_0_, ...), custom_call_target="tpu_custom_call" | custom-call | tf_op jit(solution)/shard_map/sum_tiles/pallas_call | solution.py:142
  (62 shorter events, 0.7 us)
Async XLA Ops:
  1.0 18.5 %collective-permute-start = (bf16[64,2304]{1,0:T(8,128)(2,1)S(1)}, bf16[64,2304]{1,0:T(8,128)(2,1)S(1)}, u32[]{:S(2)}, u32[]{:S(2)}) collective-permute-start(bf16[64,2304]{1,0:T(8,128)(2,1)S(1)} %pad_maximum_fusion.1.x0_ref), channel_id=1, source_target_pairs={{0,1},{1,2},{2,3},{3,0},{4,5},{5,6},{6,7},{7,4},{8,9},{9,10},{10,1... | collective-permute-start | bytes 884744 | tf_op jit(solution)/shard_map/ppermute | solution.py:204
  3.1 16.3 %collective-permute-start.1 = (bf16[64,2304]{1,0:T(8,128)(2,1)S(1)}, bf16[64,2304]{1,0:T(8,128)(2,1)S(1)}, u32[]{:S(2)}, u32[]{:S(2)}) collective-permute-start(bf16[64,2304]{1,0:T(8,128)(2,1)S(1)} %pad_maximum_fusion.1.x0_ref), channel_id=1, source_target_pairs={{0,2},{1,3},{2,0},{3,1},{4,6},{5,7},{6,4},{7,5},{8,10},{9,11},{10,... | collective-permute-start | bytes 884744 | tf_op jit(solution)/shard_map/ppermute | solution.py:204
  5.6 13.9 %collective-permute-start.2 = (bf16[64,2304]{1,0:T(8,128)(2,1)S(1)}, bf16[64,2304]{1,0:T(8,128)(2,1)S(1)}, u32[]{:S(2)}, u32[]{:S(2)}) collective-permute-start(bf16[64,2304]{1,0:T(8,128)(2,1)S(1)} %pad_maximum_fusion.1.x0_ref), channel_id=1, source_target_pairs={{0,3},{1,0},{2,1},{3,2},{4,7},{5,4},{6,5},{7,6},{8,11},{9,8},{10,9... | collective-permute-start | bytes 884744 | tf_op jit(solution)/shard_map/ppermute | solution.py:204
  8.9 10.6 %all-to-all-start = ((s32[8,1,128]{2,1,0:T(1,128)}), s32[8,1,128]{2,1,0:T(1,128)S(1)}, u32[]{:S(2)}, u32[]{:S(2)}) async-start(s32[8,1,128]{2,1,0:T(1,128)} %bitcast.3), calls=%async_computation | async-start | bytes 8192 | tf_op jit(solution)/shard_map/all_to_all | solution.py:224
  19.5 27.1 %copy-start.4 = (f32[64]{0:T(128)S(1)}, f32[64]{0:T(128)}, u32[]{:S(2)}) copy-start(f32[64]{0:T(128)} %param.10) | copy-start | bytes 772
  21.4 12.8 %collective-permute-start.3 = (bf16[16,64,128]{2,1,0:T(8,128)(2,1)S(1)}, bf16[16,64,128]{2,1,0:T(8,128)(2,1)S(1)}, u32[]{:S(2)}, u32[]{:S(2)}) collective-permute-start(bf16[16,64,128]{2,1,0:T(8,128)(2,1)S(1)} %hidden_blocks.1.refs_0_), channel_id=1, source_target_pairs={{0,8},{4,12},{8,0},{12,4},{16,24},{20,28},{24,16},{28,20},{32,40},... | collective-permute-start | bytes 786440 | tf_op jit(solution)/shard_map/ppermute | solution.py:192
  23.1 11.1 %collective-permute-start.4 = (bf16[16,64,128]{2,1,0:T(8,128)(2,1)S(1)}, bf16[16,64,128]{2,1,0:T(8,128)(2,1)S(1)}, u32[]{:S(2)}, u32[]{:S(2)}) collective-permute-start(bf16[16,64,128]{2,1,0:T(8,128)(2,1)S(1)} %hidden_blocks.1.refs_0_), channel_id=1, source_target_pairs={{0,56},{4,60},{8,16},{12,20},{16,8},{20,12},{24,32},{28,36},{32,24... | collective-permute-start | bytes 786440 | tf_op jit(solution)/shard_map/ppermute | solution.py:192
  27.8 2.2 %copy-start.2 = (bf16[16,8,128,128]{3,2,1,0:T(8,128)(2,1)S(1)}, bf16[16,8,128,128]{3,2,1,0:T(8,128)(2,1)}, u32[]{:S(2)}) copy-start(bf16[16,8,128,128]{3,2,1,0:T(8,128)(2,1)} %tiles_ref.1) | copy-start | bytes 12582916
  30.0 0.7 copy-start.3
  32.3 2.0 %copy-start = (bf16[16,8,128,128]{3,2,1,0:T(8,128)(2,1)}, bf16[16,8,128,128]{3,2,1,0:T(8,128)(2,1)S(1)}, u32[]{:S(2)}) copy-start(bf16[16,8,128,128]{3,2,1,0:T(8,128)(2,1)S(1)} %load_tiles.1.tiles_ref) | copy-start | bytes 12582916
  34.2 6.7 %collective-permute-start.10 = (bf16[16,64,128]{2,1,0:T(8,128)(2,1)S(1)}, bf16[16,64,128]{2,1,0:T(8,128)(2,1)S(1)}, u32[]{:S(2)}, u32[]{:S(2)}) collective-permute-start(bf16[16,64,128]{2,1,0:T(8,128)(2,1)S(1)} %collective-permute-done.4.refs_1_), channel_id=1, source_target_pairs={{0,8},{4,12},{8,0},{12,4},{16,24},{20,28},{24,16},{28,20},{32,40},... | collective-permute-start | bytes 786440 | tf_op jit(solution)/shard_map/ppermute | solution.py:192
  34.2 8.0 %collective-permute-start.9 = (bf16[16,64,128]{2,1,0:T(8,128)(2,1)S(1)}, bf16[16,64,128]{2,1,0:T(8,128)(2,1)S(1)}, u32[]{:S(2)}, u32[]{:S(2)}) collective-permute-start(bf16[16,64,128]{2,1,0:T(8,128)(2,1)S(1)} %collective-permute-done.3.refs_0_), channel_id=1, source_target_pairs={{0,56},{4,60},{8,16},{12,20},{16,8},{20,12},{24,32},{28,36},{32,24... | collective-permute-start | bytes 786440 | tf_op jit(solution)/shard_map/ppermute | solution.py:192
  36.7 6.9 %collective-permute-start.5 = (bf16[2,2,2,64,128]{4,3,2,1,0:T(8,128)(2,1)S(1)}, bf16[2,2,2,64,128]{4,3,2,1,0:T(8,128)(2,1)S(1)}, u32[]{:S(2)}, u32[]{:S(2)}) collective-permute-start(bf16[2,2,2,64,128]{4,3,2,1,0:T(8,128)(2,1)S(1)} %get-tuple-element.43), channel_id=1, source_target_pairs={{0,64},{4,68},{8,72},{12,76},{16,80},{20,84},{24,88},{28,92},{32,9... | collective-permute-start | bytes 393224 | tf_op jit(solution)/shard_map/ppermute | solution.py:192
  37.0 6.6 %collective-permute-start.6 = (bf16[2,2,2,64,128]{4,3,2,1,0:T(8,128)(2,1)S(1)}, bf16[2,2,2,64,128]{4,3,2,1,0:T(8,128)(2,1)S(1)}, u32[]{:S(2)}, u32[]{:S(2)}) collective-permute-start(bf16[2,2,2,64,128]{4,3,2,1,0:T(8,128)(2,1)S(1)} %get-tuple-element.44), channel_id=1, source_target_pairs={{0,128},{4,132},{8,136},{12,140},{16,144},{20,148},{24,152},{28,15... | collective-permute-start | bytes 393224 | tf_op jit(solution)/shard_map/ppermute | solution.py:192
  39.3 6.3 %collective-permute-start.7 = (bf16[2,2,2,64,128]{4,3,2,1,0:T(8,128)(2,1)S(1)}, bf16[2,2,2,64,128]{4,3,2,1,0:T(8,128)(2,1)S(1)}, u32[]{:S(2)}, u32[]{:S(2)}) collective-permute-start(bf16[2,2,2,64,128]{4,3,2,1,0:T(8,128)(2,1)S(1)} %get-tuple-element.45), channel_id=1, source_target_pairs={{0,192},{4,196},{8,200},{12,204},{16,208},{20,212},{24,216},{28,22... | collective-permute-start | bytes 393224 | tf_op jit(solution)/shard_map/ppermute | solution.py:192
  40.9 6.4 %collective-permute-start.15 = (bf16[16,64,128]{2,1,0:T(8,128)(2,1)S(1)}, bf16[16,64,128]{2,1,0:T(8,128)(2,1)S(1)}, u32[]{:S(2)}, u32[]{:S(2)}) collective-permute-start(bf16[16,64,128]{2,1,0:T(8,128)(2,1)S(1)} %collective-permute-done.10.refs_2_), channel_id=1, source_target_pairs={{0,56},{4,60},{8,16},{12,20},{16,8},{20,12},{24,32},{28,36},{32,24... | collective-permute-start | bytes 786440 | tf_op jit(solution)/shard_map/ppermute | solution.py:192
  42.2 5.7 %collective-permute-start.16 = (bf16[16,64,128]{2,1,0:T(8,128)(2,1)S(1)}, bf16[16,64,128]{2,1,0:T(8,128)(2,1)S(1)}, u32[]{:S(2)}, u32[]{:S(2)}) collective-permute-start(bf16[16,64,128]{2,1,0:T(8,128)(2,1)S(1)} %collective-permute-done.9.refs_1_), channel_id=1, source_target_pairs={{0,8},{4,12},{8,0},{12,4},{16,24},{20,28},{24,16},{28,20},{32,40},... | collective-permute-start | bytes 786440 | tf_op jit(solution)/shard_map/ppermute | solution.py:192
  43.6 8.7 %collective-permute-start.11 = (bf16[2,3,2,64,128]{4,3,2,1,0:T(8,128)(2,1)S(1)}, bf16[2,3,2,64,128]{4,3,2,1,0:T(8,128)(2,1)S(1)}, u32[]{:S(2)}, u32[]{:S(2)}) collective-permute-start(bf16[2,3,2,64,128]{4,3,2,1,0:T(8,128)(2,1)S(1)} %get-tuple-element.49), channel_id=1, source_target_pairs={{0,64},{4,68},{8,72},{12,76},{16,80},{20,84},{24,88},{28,92},{32,9... | collective-permute-start | bytes 589832 | tf_op jit(solution)/shard_map/ppermute | solution.py:192
  43.6 8.7 %collective-permute-start.12 = (bf16[2,3,2,64,128]{4,3,2,1,0:T(8,128)(2,1)S(1)}, bf16[2,3,2,64,128]{4,3,2,1,0:T(8,128)(2,1)S(1)}, u32[]{:S(2)}, u32[]{:S(2)}) collective-permute-start(bf16[2,3,2,64,128]{4,3,2,1,0:T(8,128)(2,1)S(1)} %get-tuple-element.50), channel_id=1, source_target_pairs={{0,128},{4,132},{8,136},{12,140},{16,144},{20,148},{24,152},{28,15... | collective-permute-start | bytes 589832 | tf_op jit(solution)/shard_map/ppermute | solution.py:192
  45.6 7.3 %collective-permute-start.13 = (bf16[2,3,2,64,128]{4,3,2,1,0:T(8,128)(2,1)S(1)}, bf16[2,3,2,64,128]{4,3,2,1,0:T(8,128)(2,1)S(1)}, u32[]{:S(2)}, u32[]{:S(2)}) collective-permute-start(bf16[2,3,2,64,128]{4,3,2,1,0:T(8,128)(2,1)S(1)} %get-tuple-element.51), channel_id=1, source_target_pairs={{0,192},{4,196},{8,200},{12,204},{16,208},{20,212},{24,216},{28,22... | collective-permute-start | bytes 589832 | tf_op jit(solution)/shard_map/ppermute | solution.py:192
  46.7 24.3 %copy-start.1 = (bf16[16,8,128,128]{3,2,1,0:T(8,128)(2,1)S(1)}, bf16[16,8,128,128]{3,2,1,0:T(8,128)(2,1)}, u32[]{:S(2)}) copy-start(bf16[16,8,128,128]{3,2,1,0:T(8,128)(2,1)} %copy-done) | copy-start | bytes 12582916
  47.3 7.9 %collective-permute-start.21 = (bf16[8,64,128]{2,1,0:T(8,128)(2,1)S(1)}, bf16[8,64,128]{2,1,0:T(8,128)(2,1)S(1)}, u32[]{:S(2)}, u32[]{:S(2)}) collective-permute-start(bf16[8,64,128]{2,1,0:T(8,128)(2,1)S(1)} %slice.65), channel_id=1, source_target_pairs={{0,8},{4,12},{8,0},{12,4},{16,24},{20,28},{24,16},{28,20},{32,40},... | collective-permute-start | bytes 393224 | tf_op jit(solution)/shard_map/ppermute | solution.py:192
  47.9 12.5 %collective-permute-start.22 = (bf16[8,64,128]{2,1,0:T(8,128)(2,1)S(1)}, bf16[8,64,128]{2,1,0:T(8,128)(2,1)S(1)}, u32[]{:S(2)}, u32[]{:S(2)}) collective-permute-start(bf16[8,64,128]{2,1,0:T(8,128)(2,1)S(1)} %slice.66), channel_id=1, source_target_pairs={{0,56},{4,60},{8,16},{12,20},{16,8},{20,12},{24,32},{28,36},{32,24... | collective-permute-start | bytes 393224 | tf_op jit(solution)/shard_map/ppermute | solution.py:192
  52.3 8.9 %collective-permute-start.17 = (bf16[2,2,2,64,128]{4,3,2,1,0:T(8,128)(2,1)S(1)}, bf16[2,2,2,64,128]{4,3,2,1,0:T(8,128)(2,1)S(1)}, u32[]{:S(2)}, u32[]{:S(2)}) collective-permute-start(bf16[2,2,2,64,128]{4,3,2,1,0:T(8,128)(2,1)S(1)} %get-tuple-element.54), channel_id=1, source_target_pairs={{0,64},{4,68},{8,72},{12,76},{16,80},{20,84},{24,88},{28,92},{32,9... | collective-permute-start | bytes 393224 | tf_op jit(solution)/shard_map/ppermute | solution.py:192
  52.3 9.6 %collective-permute-start.18 = (bf16[2,2,2,64,128]{4,3,2,1,0:T(8,128)(2,1)S(1)}, bf16[2,2,2,64,128]{4,3,2,1,0:T(8,128)(2,1)S(1)}, u32[]{:S(2)}, u32[]{:S(2)}) collective-permute-start(bf16[2,2,2,64,128]{4,3,2,1,0:T(8,128)(2,1)S(1)} %get-tuple-element.55), channel_id=1, source_target_pairs={{0,128},{4,132},{8,136},{12,140},{16,144},{20,148},{24,152},{28,15... | collective-permute-start | bytes 393224 | tf_op jit(solution)/shard_map/ppermute | solution.py:192
  52.9 10.4 %collective-permute-start.19 = (bf16[2,2,2,64,128]{4,3,2,1,0:T(8,128)(2,1)S(1)}, bf16[2,2,2,64,128]{4,3,2,1,0:T(8,128)(2,1)S(1)}, u32[]{:S(2)}, u32[]{:S(2)}) collective-permute-start(bf16[2,2,2,64,128]{4,3,2,1,0:T(8,128)(2,1)S(1)} %get-tuple-element.56), channel_id=1, source_target_pairs={{0,192},{4,196},{8,200},{12,204},{16,208},{20,212},{24,216},{28,22... | collective-permute-start | bytes 393224 | tf_op jit(solution)/shard_map/ppermute | solution.py:192
  55.2 14.8 %collective-permute-start.8 = (bf16[4,2,2,64,128]{4,3,2,1,0:T(8,128)(2,1)S(1)}, bf16[4,2,2,64,128]{4,3,2,1,0:T(8,128)(2,1)S(1)}, u32[]{:S(2)}, u32[]{:S(2)}) collective-permute-start(bf16[4,2,2,64,128]{4,3,2,1,0:T(8,128)(2,1)S(1)} %pad_maximum_fusion.2), channel_id=1, source_target_pairs={{0,4},{4,0},{8,12},{12,8},{16,20},{20,16},{24,28},{28,24},{32,36},... | collective-permute-start | bytes 786440 | tf_op jit(solution)/shard_map/ppermute | solution.py:192
  60.4 10.5 %collective-permute-start.14 = (bf16[4,3,2,64,128]{4,3,2,1,0:T(8,128)(2,1)S(1)}, bf16[4,3,2,64,128]{4,3,2,1,0:T(8,128)(2,1)S(1)}, u32[]{:S(2)}, u32[]{:S(2)}) collective-permute-start(bf16[4,3,2,64,128]{4,3,2,1,0:T(8,128)(2,1)S(1)} %pad_maximum_fusion), channel_id=1, source_target_pairs={{0,4},{4,0},{8,12},{12,8},{16,20},{20,16},{24,28},{28,24},{32,36},... | collective-permute-start | bytes 1179656 | tf_op jit(solution)/shard_map/ppermute | solution.py:192
  61.2 4.4 %collective-permute-start.23 = (bf16[2,1,2,64,128]{4,3,2,1,0:T(8,128)(2,1)S(1)}, bf16[2,1,2,64,128]{4,3,2,1,0:T(8,128)(2,1)S(1)}, u32[]{:S(2)}, u32[]{:S(2)}) collective-permute-start(bf16[2,1,2,64,128]{4,3,2,1,0:T(8,128)(2,1)S(1)} %get-tuple-element.59), channel_id=1, source_target_pairs={{0,64},{4,68},{8,72},{12,76},{16,80},{20,84},{24,88},{28,92},{32,9... | collective-permute-start | bytes 196616 | tf_op jit(solution)/shard_map/ppermute | solution.py:192
  61.9 6.1 %collective-permute-start.24 = (bf16[2,1,2,64,128]{4,3,2,1,0:T(8,128)(2,1)S(1)}, bf16[2,1,2,64,128]{4,3,2,1,0:T(8,128)(2,1)S(1)}, u32[]{:S(2)}, u32[]{:S(2)}) collective-permute-start(bf16[2,1,2,64,128]{4,3,2,1,0:T(8,128)(2,1)S(1)} %get-tuple-element.60), channel_id=1, source_target_pairs={{0,128},{4,132},{8,136},{12,140},{16,144},{20,148},{24,152},{28,15... | collective-permute-start | bytes 196616 | tf_op jit(solution)/shard_map/ppermute | solution.py:192
  63.3 4.8 %collective-permute-start.25 = (bf16[2,1,2,64,128]{4,3,2,1,0:T(8,128)(2,1)S(1)}, bf16[2,1,2,64,128]{4,3,2,1,0:T(8,128)(2,1)S(1)}, u32[]{:S(2)}, u32[]{:S(2)}) collective-permute-start(bf16[2,1,2,64,128]{4,3,2,1,0:T(8,128)(2,1)S(1)} %get-tuple-element.61), channel_id=1, source_target_pairs={{0,192},{4,196},{8,200},{12,204},{16,208},{20,212},{24,216},{28,22... | collective-permute-start | bytes 196616 | tf_op jit(solution)/shard_map/ppermute | solution.py:192
  65.6 5.3 %collective-permute-start.20 = (bf16[4,2,2,64,128]{4,3,2,1,0:T(8,128)(2,1)S(1)}, bf16[4,2,2,64,128]{4,3,2,1,0:T(8,128)(2,1)S(1)}, u32[]{:S(2)}, u32[]{:S(2)}) collective-permute-start(bf16[4,2,2,64,128]{4,3,2,1,0:T(8,128)(2,1)S(1)} %pad_maximum_fusion.3), channel_id=1, source_target_pairs={{0,4},{4,0},{8,12},{12,8},{16,20},{20,16},{24,28},{28,24},{32,36},... | collective-permute-start | bytes 786440 | tf_op jit(solution)/shard_map/ppermute | solution.py:192
  68.1 2.8 %collective-permute-start.26 = (bf16[4,1,2,64,128]{4,3,2,1,0:T(8,128)(2,1)S(1)}, bf16[4,1,2,64,128]{4,3,2,1,0:T(8,128)(2,1)S(1)}, u32[]{:S(2)}, u32[]{:S(2)}) collective-permute-start(bf16[4,1,2,64,128]{4,3,2,1,0:T(8,128)(2,1)S(1)} %pad_maximum_fusion.4), channel_id=1, source_target_pairs={{0,4},{4,0},{8,12},{12,8},{16,20},{20,16},{24,28},{28,24},{32,36},... | collective-permute-start | bytes 393224 | tf_op jit(solution)/shard_map/ppermute | solution.py:192
